TPU v7x, 256 devices: a whole 4x4x8 slice. The times are simulated.
256 devices in a mesh: pair: 64 (over y, x_hi, z), row: 4 (over x_lo, core).
Axes of the slice: x: 4 (x_hi: 2, x_lo: 2; x = x_hi * 2 + x_lo), y: 4, z: 8, core: 2. Of those that a mesh axis runs over, the one named last changes fastest.
Arguments:
- matrix: float32 [16384, 16384], P('row', 'pair')
- plan: int32 [2], replicated, may hold values from 1 to 63, as said below
Outputs:
- final_matrix: float32 [16384, 16384], P('row', 'pair')
Inputs may be any that keep to these rules, and one draw needn't show every extreme that they name: Round r pairs pair index p with p XOR plan[r]; the 2 masks are distinct and one of them equals 63.
All inputs are finite; a program needn't handle non-finite values.
Results may differ from a plain program's by a relative error of at most 0.0003.
Values sent between devices are 32-bit elements; how exact they have to be, the bound alone decides.
A program may use at most 64 MiB of HBM per device.

v0:
```python
import functools
import jax
import jax.numpy as jnp
from jax import lax
from jax.experimental import pallas as pl
from jax.experimental.pallas import tpu as pltpu
from jax.sharding import PartitionSpec as P

F32 = jnp.float32
BF16 = jnp.bfloat16
B = 128
SETS = 16


def lanes(shape):
    return lax.broadcasted_iota(jnp.int32, shape, len(shape) - 1)


def lane_gather(x, index):
    return jnp.take_along_axis(x, jnp.broadcast_to(index, x.shape), axis=1, mode="promise_in_bounds")


def shift_lanes(top, bottom):
    lane = lanes(top.shape)
    new_top = jnp.where(lane == B - 1, bottom, pltpu.roll(top, B - 1, 1))
    new_bottom = jnp.where(lane == 0, bottom, pltpu.roll(jnp.where(lane == 0, top, bottom), 1, 1))
    return new_top, new_bottom


def angles(first, second, coupling, step):
    lane = lanes(first.shape)
    top_is_lower = (lane == 0) | (lane > step)
    difference = second - first
    forward = (difference > 0) | ((difference == 0) & top_is_lower)
    tangent = jnp.where(forward, 2.0, -2.0) * coupling / (
        jnp.abs(difference)
        + jnp.sqrt(difference * difference + 4.0 * coupling * coupling)
        + 1e-06 * (first + second)
    )
    cosine = 1.0 / jnp.sqrt(1.0 + tangent * tangent)
    return cosine, cosine * tangent


def one_set(step, p, grams, v_top, v_bot):
    tt, tb, bt, bb = grams
    q = 1 - p
    eye = lax.broadcasted_iota(jnp.int32, (B, B), 0) == lanes((B, B))
    diag = lambda ref, base: jnp.sum(jnp.where(eye, ref[p, base : base + B, :], 0.0), axis=0, keepdims=True)
    cosine, sine = angles(diag(tt, 1), diag(bb, 7), diag(tb, 1), step)
    col_c = jnp.broadcast_to(cosine, (B, B)).T
    col_s = jnp.broadcast_to(sine, (B, B)).T
    n = 32
    for k in range(0, B, n):
        a, b = tt[p, 1 + k : 1 + k + n, :], tb[p, 1 + k : 1 + k + n, :]
        c, d = bt[p, 7 + k : 7 + k + n, :], bb[p, 7 + k : 7 + k + n, :]
        a, b = cosine * a - sine * b, cosine * b + sine * a
        c, d = cosine * c - sine * d, cosine * d + sine * c
        cc, ss = col_c[k : k + n], col_s[k : k + n]
        a, c = cc * a - ss * c, cc * c + ss * a
        b, d = cc * b - ss * d, cc * d + ss * b
        a, b = shift_lanes(a, b)
        c, d = shift_lanes(c, d)
        tt[q, k : k + n, :], tb[q, k : k + n, :] = a, b
        bt[q, 8 + k : 8 + k + n, :], bb[q, 8 + k : 8 + k + n, :] = c, d
    for top, bottom in ((tt, bt), (tb, bb)):
        first = bottom[q, 8:9, :]
        top[q, B : B + 1, :] = bottom[q, B + 7 : B + 8, :]
        bottom[q, 7:8, :] = first
        bottom[q, 8:9, :] = top[q, 0:1, :]
    for k in range(0, 2 * B, n):
        a, b = v_top[k : k + n, :], v_bot[k : k + n, :]
        a, b = shift_lanes(cosine * a - sine * b, cosine * b + sine * a)
        v_top[k : k + n, :], v_bot[k : k + n, :] = a, b


def jacobi(ll, lr, rr, grams, v_top, v_bot):
    tt, tb, bt, bb = grams
    lane = lanes((1, B))
    lr = lane_gather(lr, B - 1 - lane)
    rr = lane_gather(lane_gather(rr, B - 1 - lane).T, B - 1 - lane)
    tt[0, 1 : B + 1, :] = ll
    tb[0, 1 : B + 1, :] = lr
    bt[0, 7 : B + 7, :] = lr.T
    bb[0, 7 : B + 7, :] = rr
    row = lax.broadcasted_iota(jnp.int32, (2 * B, B), 0)
    v_top[...] = jnp.where(row == lanes((2 * B, B)), 1.0, 0.0)
    v_bot[...] = jnp.where(row + lanes((2 * B, B)) == 2 * B - 1, 1.0, 0.0)

    @pl.loop(0, SETS // 2)
    def _(i):
        one_set(2 * i, 0, grams, v_top, v_bot)
        one_set(2 * i + 1, 1, grams, v_top, v_bot)

    top, bottom = v_top[...], v_bot[...]
    lane = lanes((1, B))
    moved = pltpu.roll(top, SETS, 1)
    low = lane < SETS
    left = jnp.where(low, lane_gather(bottom, (SETS - lane) & (B - 1)), moved)
    right = jnp.where(low, moved, lane_gather(bottom, jnp.where(lane == B - 1, 0, (B + SETS - 1 - lane) & (B - 1))))
    return left, right

ROWS = 4096
CHUNK = 512
CHUNKS = ROWS // CHUNK
MESH = pl.DeviceIdType.MESH


def split(x):
    high = x.astype(BF16)
    return high, (x - high.astype(F32)).astype(BF16)


def gram_blocks(y, products, squares, arrive):
    products[...] = jnp.zeros_like(products)
    squares[...] = jnp.zeros_like(squares)

    @pl.loop(0, CHUNKS)
    def _(i):
        arrive(i)
        x = y[pl.ds(i * CHUNK, CHUNK), :]
        high, low = split(x)
        products[...] += lax.dot_general(
            high, jnp.concatenate([high, low], axis=1), (((0,), (0,)), ((), ())), preferred_element_type=F32
        )
        small = low.astype(F32)
        squares[...] += jnp.sum((small * small).reshape(CHUNK // 8, 8, 2 * B), axis=0)

    eye = lax.broadcasted_iota(jnp.int32, (B, B), 0) == lanes((B, B))
    low_square = jnp.sum(squares[...], axis=0, keepdims=True)
    ll = products[:B, 2 * B : 3 * B]
    lr = products[:B, 3 * B :]
    rl = products[B:, 2 * B : 3 * B]
    rr = products[B:, 3 * B :]
    return (
        products[:B, :B] + (ll + ll.T) + jnp.where(eye, low_square[:, :B], 0.0),
        products[:B, B : 2 * B] + (lr + rl.T),
        products[B:, B : 2 * B] + (rr + rr.T) + jnp.where(eye, low_square[:, B:], 0.0),
    )


HALF = 3 * B // 2


def row_sum(part, recv_a, acc, recv_b, full, send, recv):
    pair, row = lax.axis_index("pair"), lax.axis_index("row")
    core, chip = lax.rem(row, 2), lax.div(row, 2)
    mate = (pair, 2 * chip + 1 - core)
    across = (pair, 2 * (1 - chip) + core)
    mine, other = pl.ds(core * HALF, HALF), pl.ds((1 - core) * HALF, HALF)

    def copy(k, src, dst, device):
        return pltpu.make_async_remote_copy(
            src_ref=src, dst_ref=dst, send_sem=send.at[k], recv_sem=recv.at[k], device_id=device, device_id_type=MESH
        )

    pl.semaphore_wait(pltpu.get_barrier_semaphore(), 2)
    first = copy(0, part.at[other, :], recv_a, mate)
    first.start()
    first.wait()
    acc[...] = part[mine, :] + recv_a[...]
    second = copy(1, acc, recv_b, across)
    second.start()
    second.wait()
    full[mine, :] = acc[...] + recv_b[...]
    third = copy(2, full.at[mine, :], full.at[mine, :], mate)
    third.start()
    third.wait()


def announce():
    pair, row = lax.axis_index("pair"), lax.axis_index("row")
    core, chip = lax.rem(row, 2), lax.div(row, 2)
    barrier = pltpu.get_barrier_semaphore()
    for device in ((pair, 2 * chip + 1 - core), (pair, 2 * (1 - chip) + core)):
        pl.semaphore_signal(barrier, inc=1, device_id=device, device_id_type=MESH)


def round_kernel(whole, *refs):
    ins, refs = (refs[:1], refs[1:]) if whole else (refs[:2], refs[2:])
    left_out, right_out, y, products, squares, part, recv_a, acc, recv_b, full, v_high, v_low = refs[:12]
    grams, (v_top, v_bot), (load, store, send, recv) = refs[12:16], refs[16:18], refs[18:]
    announce()

    def loads(i):
        rows = pl.ds(i * CHUNK, CHUNK)
        if whole:
            return [pltpu.make_async_copy(ins[0].at[rows, :], y.at[rows, :], load.at[i, 0])]
        return [
            pltpu.make_async_copy(ins[0].at[rows, :], y.at[rows, pl.ds(0, B)], load.at[i, 0]),
            pltpu.make_async_copy(ins[1].at[rows, :], y.at[rows, pl.ds(B, B)], load.at[i, 1]),
        ]

    def stores(i):
        rows = pl.ds(i * CHUNK, CHUNK)
        return [
            pltpu.make_async_copy(y.at[rows, pl.ds(0, B)], left_out.at[rows, :], store.at[i, 0]),
            pltpu.make_async_copy(y.at[rows, pl.ds(B, B)], right_out.at[rows, :], store.at[i, 1]),
        ]

    for i in range(CHUNKS):
        for c in loads(i):
            c.start()

    def arrive(i):
        for c in loads(i):
            c.wait()

    part[:B, :], part[B : 2 * B, :], part[2 * B :, :] = gram_blocks(y, products, squares, arrive)
    row_sum(part, recv_a, acc, recv_b, full, send, recv)
    left, right = jacobi(full[:B, :], full[B : 2 * B, :], full[2 * B :, :], grams, v_top, v_bot)
    v_high[:, :B], v_low[:, :B] = split(left)
    v_high[:, B:], v_low[:, B:] = split(right)

    @pl.loop(0, CHUNKS)
    def _(i):
        rows = pl.ds(i * CHUNK, CHUNK)
        high, low = split(y[rows, :])
        dot = functools.partial(jnp.dot, preferred_element_type=F32)
        y[rows, :] = dot(high, v_high[...]) + (dot(high, v_low[...]) + dot(low, v_high[...]))
        for c in stores(i):
            c.start()

    @pl.loop(0, CHUNKS)
    def _(i):
        for c in stores(i):
            c.wait()


def one_round(index, ins):
    flops = 2 * ROWS * (2 * B) ** 2 * 5
    return pl.pallas_call(
        functools.partial(round_kernel, len(ins) == 1),
        out_shape=(jax.ShapeDtypeStruct((ROWS, B), F32),) * 2,
        in_specs=[pl.BlockSpec(memory_space=pl.ANY)] * len(ins),
        out_specs=(pl.BlockSpec(memory_space=pl.ANY), pl.BlockSpec(memory_space=pl.ANY)),
        scratch_shapes=[
            pltpu.VMEM((ROWS, 2 * B), F32),
            pltpu.VMEM((2 * B, 4 * B), F32),
            pltpu.VMEM((8, 2 * B), F32),
            pltpu.VMEM((3 * B, B), F32),
            pltpu.VMEM((HALF, B), F32),
            pltpu.VMEM((HALF, B), F32),
            pltpu.VMEM((HALF, B), F32),
            pltpu.VMEM((3 * B, B), F32),
            pltpu.VMEM((2 * B, 2 * B), BF16),
            pltpu.VMEM((2 * B, 2 * B), BF16),
        ]
        + [pltpu.VMEM((2, B + 16, B), F32) for _ in range(4)]
        + [pltpu.VMEM((2 * B, B), F32) for _ in range(2)]
        + [
            pltpu.SemaphoreType.DMA((CHUNKS, 2)),
            pltpu.SemaphoreType.DMA((CHUNKS, 2)),
            pltpu.SemaphoreType.DMA((3,)),
            pltpu.SemaphoreType.DMA((3,)),
        ],
        compiler_params=pltpu.CompilerParams(
            collective_id=index, has_side_effects=True, vmem_limit_bytes=40 * 2**20
        ),
        cost_estimate=pl.CostEstimate(flops=flops, bytes_accessed=4 * ROWS * B * 4, transcendentals=0),
        name="round",
    )(*ins)


PARTS = 4


def transfer_kernel(mask, block, out, send, recv):
    to = (jnp.bitwise_xor(lax.axis_index("pair"), mask), lax.axis_index("row"))
    barrier = pltpu.get_barrier_semaphore()
    pl.semaphore_signal(barrier, inc=1, device_id=to, device_id_type=MESH)
    pl.semaphore_wait(barrier, 1)
    copies = []
    for i in range(PARTS):
        rows = pl.ds(i * (ROWS // PARTS), ROWS // PARTS)
        copies.append(
            pltpu.make_async_remote_copy(
                src_ref=block.at[rows, :],
                dst_ref=out.at[rows, :],
                send_sem=send.at[i],
                recv_sem=recv.at[i],
                device_id=to,
                device_id_type=MESH,
            )
        )
    for c in copies:
        c.start()
    for c in copies:
        c.wait()


def transfer(mask, block):
    if mask == 0:
        return block
    return pl.pallas_call(
        functools.partial(transfer_kernel, mask),
        out_shape=jax.ShapeDtypeStruct(block.shape, block.dtype),
        in_specs=[pl.BlockSpec(memory_space=pl.ANY)],
        out_specs=pl.BlockSpec(memory_space=pl.ANY),
        scratch_shapes=[pltpu.SemaphoreType.DMA((PARTS,)), pltpu.SemaphoreType.DMA((PARTS,))],
        compiler_params=pltpu.CompilerParams(collective_id=mask, has_side_effects=True),
        cost_estimate=pl.CostEstimate(flops=0, bytes_accessed=2 * ROWS * B * 4, transcendentals=0),
        name="transfer",
    )(block)


LOW_BITS = 3


def route(block, mask):
    count = lax.axis_size("pair")
    low_count = 1 << LOW_BITS

    def high_part(high, block):
        return lax.switch(
            jnp.bitwise_and(mask, low_count - 1),
            [functools.partial(transfer, high * low_count + low) for low in range(low_count)],
            block,
        )

    return lax.switch(
        jnp.right_shift(mask, LOW_BITS), [functools.partial(high_part, h) for h in range(count // low_count)], block
    )


def local(matrix, plan):
    left, right = one_round(64, (matrix,))
    right = route(right, plan[0])
    left, right = one_round(65, (left, right))
    return jnp.concatenate([left, route(right, plan[1])], axis=1)


def solution(mesh):
    return jax.shard_map(
        local, mesh=mesh, in_specs=(P("row", "pair"), P()), out_specs=P("row", "pair"), check_vma=False
    )
```

profile of v0, /device:TPU:1, one launch (start us, length us, event | category | flops | bytes accessed | tf_op | source)
XLA Modules:
  0.0 295.9 jit_solution(3353167590402133645)
XLA Ops:
  0.0 1.4 fusion
  1.4 0.0 copy-start
  1.4 2.2 copy-done
  3.6 33.8 %round.2 = (f32[4096,128]{1,0:T(8,128)S(1)}, f32[4096,128]{1,0:T(8,128)S(1)}) custom-call(f32[4096,256]{1,0:T(8,128)S(1)} %copy-done), custom_call_target="tpu_custom_call" | custom-call | flops 2684354560 | bytes 8388608 | tf_op jit(solution)/shard_map/round/pallas_call | solution.py:231
  37.4 0.0 copy-start.1
  37.4 1.3 copy-done.1
  39.4 113.7 %conditional.18 = (f32[4096,128]{1,0:T(8,128)S(1)}) conditional(s32[]{:T(128)} %clamp.54, (s32[]{:T(128)}, f32[4096,128]{1,0:T(8,128)S(1)}) %tuple.437, (s32[]{:T(128)}, f32[4096,128]{1,0:T(8,128)S(1)}) %tuple.437, (s32[]{:T(128)}, f32[4096,128]{1,0:T(8,128)S(1)}) %tuple.437, (s32[]{:T(128)}, ...), branch_computations={%region_0.0_spmd, %region_9.0_spmd, %region_18.0_spmd, %region_27.... | conditional | flops 2 | bytes 8388652 | solution.py:320
  40.3 111.2 %conditional.7 = (f32[4096,128]{1,0:T(8,128)}) conditional(s32[]{:T(128)} %clamp.43, f32[4096,128]{1,0:T(8,128)S(1)} %get-tuple-element.374, f32[4096,128]{1,0:T(8,128)S(1)} %get-tuple-element.374, f32[4096,128]{1,0:T(8,128)S(1)} %get-tuple-element.374, f32[4096,128]{1,0:T(8,128)S(1)} %get-tuple-element.374, ...), branch_computations={%region_64.0_spmd, %region_65.0_spmd, %region_66.0_spmd, %region_6... | conditional | bytes 4194312 | solution.py:314
  40.4 111.1 %transfer.188 = f32[4096,128]{1,0:T(8,128)} custom-call(f32[4096,128]{1,0:T(8,128)S(1)} %block.55), custom_call_target="tpu_custom_call" | custom-call | bytes 4194304 | tf_op jit(solution)/shard_map/cond/branch_7_fun/cond/branch_7_fun/transfer/pallas_call | solution.py:294
  151.5 1.6 copy.138
  153.1 0.0 copy-start.3
  153.1 1.3 copy-done.3
  154.4 0.0 copy-start.2
  154.4 1.6 copy-done.2
  156.0 31.5 %round.3 = (f32[4096,128]{1,0:T(8,128)S(1)}, f32[4096,128]{1,0:T(8,128)}) custom-call(f32[4096,128]{1,0:T(8,128)S(1)} %copy-done.2, f32[4096,128]{1,0:T(8,128)} %copy-done.3), custom_call_target="tpu_custom_call" | custom-call | flops 2684354560 | bytes 8388608 | tf_op jit(solution)/shard_map/round/pallas_call | solution.py:231
  188.1 103.9 %conditional.19 = (f32[4096,128]{1,0:T(8,128)}) conditional(s32[]{:T(128)} %clamp.55, (s32[]{:T(128)}, f32[4096,128]{1,0:T(8,128)}) %tuple.438, (s32[]{:T(128)}, f32[4096,128]{1,0:T(8,128)}) %tuple.438, (s32[]{:T(128)}, f32[4096,128]{1,0:T(8,128)}) %tuple.438, (s32[]{:T(128)}, f32[4096,128]{1,0:T(8,128)}) %tuple.438, ...), branch_computations={%region_72.0_spmd, %region_81.0_spmd, %region_90.0_spmd, %region_9... | conditional | flops 2 | bytes 8388652 | solution.py:320
  188.9 100.1 %conditional.11 = (f32[4096,128]{1,0:T(8,128)}) conditional(s32[]{:T(128)} %clamp.47, f32[4096,128]{1,0:T(8,128)} %get-tuple-element.382, f32[4096,128]{1,0:T(8,128)} %get-tuple-element.382, f32[4096,128]{1,0:T(8,128)} %get-tuple-element.382, f32[4096,128]{1,0:T(8,128)} %get-tuple-element.382, ...), branch_computations={%region_100.0_spmd, %region_101.0_spmd, %region_102.0_spmd, %regio... | conditional | bytes 4194312 | solution.py:314
  188.9 100.1 %transfer.216 = f32[4096,128]{1,0:T(8,128)} custom-call(f32[4096,128]{1,0:T(8,128)} %block.76), custom_call_target="tpu_custom_call" | custom-call | bytes 4194304 | tf_op jit(solution)/shard_map/cond/branch_3_fun/cond/branch_4_fun/transfer/pallas_call | solution.py:294
  289.0 3.1 %copy.142 = f32[4096,128]{1,0:T(8,128)} copy(f32[4096,128]{1,0:T(8,128)} %get-tuple-element.412) | data formatting | bytes 4194304 | tf_op jit(solution)/shard_map/cond
  292.0 3.9 %pad_maximum_fusion = f32[4096,256]{1,0:T(8,128)} fusion(f32[4096,128]{1,0:T(8,128)} %get-tuple-element.418, f32[4096,128]{1,0:T(8,128)S(1)} %get-tuple-element.397), kind=kLoop, calls=%fused_computation | loop fusion | flops 1048576 | bytes 8388608 | tf_op jit(solution)/shard_map/concatenate | solution.py:329
Async XLA Ops:
  1.4 2.2 copy-start
  37.4 1.3 copy-start.1
  153.1 1.3 copy-start.3
  154.4 1.6 copy-start.2
where the time goes:
time: 297 us; the launch traced here: 296 us
  Pallas kernels  276 us (93%)
  local copies, waits for them, and re-layouts  12.4 us (4%)
  other arithmetic  3.87 us (1%)
    pallas_call x2, Pallas kernels, transfer(): pl.pallas_call(functools.partial(transfer_kernel, mask), out_shape=jax.Sh...  211 us
    pallas_call x2, Pallas kernels, one_round(): pl.pallas_call(functools.partial(round_kernel, len(ins) == 1), out_shape=...  65.3 us
    unnamed x8, local copies, waits for them, and re-layouts  6.4 us

commit v1 on v0

v1 whole, which is shorter than its diff:
```python
import functools
import jax
import jax.numpy as jnp
from jax import lax
from jax.experimental import pallas as pl
from jax.experimental.pallas import tpu as pltpu
from jax.sharding import PartitionSpec as P

F32 = jnp.float32
BF16 = jnp.bfloat16
B = 128
SETS = 16


def lanes(shape):
    return lax.broadcasted_iota(jnp.int32, shape, len(shape) - 1)


def lane_gather(x, index):
    return jnp.take_along_axis(x, jnp.broadcast_to(index, x.shape), axis=1, mode="promise_in_bounds")


def shift_lanes(top, bottom):
    lane = lanes(top.shape)
    new_top = jnp.where(lane == B - 1, bottom, pltpu.roll(top, B - 1, 1))
    new_bottom = jnp.where(lane == 0, bottom, pltpu.roll(jnp.where(lane == 0, top, bottom), 1, 1))
    return new_top, new_bottom


def angles(first, second, coupling, step):
    lane = lanes(first.shape)
    top_is_lower = (lane == 0) | (lane > step)
    difference = second - first
    forward = (difference > 0) | ((difference == 0) & top_is_lower)
    tangent = jnp.where(forward, 2.0, -2.0) * coupling / (
        jnp.abs(difference)
        + jnp.sqrt(difference * difference + 4.0 * coupling * coupling)
        + 1e-06 * (first + second)
    )
    square = 1.0 + tangent * tangent
    cosine = 1.0 / jnp.sqrt(square)
    cosine += 0.5 * cosine * (1.0 - square * cosine * cosine)
    return cosine, cosine * tangent


def one_set(step, p, grams, v_top, v_bot):
    tt, tb, bt, bb = grams
    q = 1 - p
    eye = lax.broadcasted_iota(jnp.int32, (B, B), 0) == lanes((B, B))
    diag = lambda ref, base: jnp.sum(jnp.where(eye, ref[p, base : base + B, :], 0.0), axis=0, keepdims=True)
    cosine, sine = angles(diag(tt, 1), diag(bb, 7), diag(tb, 1), step)
    col_c = jnp.broadcast_to(cosine, (B, B)).T
    col_s = jnp.broadcast_to(sine, (B, B)).T
    n = 32
    for k in range(0, B, n):
        a, b = tt[p, 1 + k : 1 + k + n, :], tb[p, 1 + k : 1 + k + n, :]
        c, d = bt[p, 7 + k : 7 + k + n, :], bb[p, 7 + k : 7 + k + n, :]
        a, b = cosine * a - sine * b, cosine * b + sine * a
        c, d = cosine * c - sine * d, cosine * d + sine * c
        cc, ss = col_c[k : k + n], col_s[k : k + n]
        a, c = cc * a - ss * c, cc * c + ss * a
        b, d = cc * b - ss * d, cc * d + ss * b
        a, b = shift_lanes(a, b)
        c, d = shift_lanes(c, d)
        tt[q, k : k + n, :], tb[q, k : k + n, :] = a, b
        bt[q, 8 + k : 8 + k + n, :], bb[q, 8 + k : 8 + k + n, :] = c, d
    for top, bottom in ((tt, bt), (tb, bb)):
        first = bottom[q, 8:9, :]
        top[q, B : B + 1, :] = bottom[q, B + 7 : B + 8, :]
        bottom[q, 7:8, :] = first
        bottom[q, 8:9, :] = top[q, 0:1, :]
    for k in range(0, 2 * B, n):
        a, b = v_top[k : k + n, :], v_bot[k : k + n, :]
        a, b = shift_lanes(cosine * a - sine * b, cosine * b + sine * a)
        v_top[k : k + n, :], v_bot[k : k + n, :] = a, b


def jacobi(ll, lr, rr, grams, v_top, v_bot):
    tt, tb, bt, bb = grams
    lane = lanes((1, B))
    lr = lane_gather(lr, B - 1 - lane)
    rr = lane_gather(lane_gather(rr, B - 1 - lane).T, B - 1 - lane)
    tt[0, 1 : B + 1, :] = ll
    tb[0, 1 : B + 1, :] = lr
    bt[0, 7 : B + 7, :] = lr.T
    bb[0, 7 : B + 7, :] = rr
    row = lax.broadcasted_iota(jnp.int32, (2 * B, B), 0)
    v_top[...] = jnp.where(row == lanes((2 * B, B)), 1.0, 0.0)
    v_bot[...] = jnp.where(row + lanes((2 * B, B)) == 2 * B - 1, 1.0, 0.0)

    @pl.loop(0, SETS // 2)
    def _(i):
        one_set(2 * i, 0, grams, v_top, v_bot)
        one_set(2 * i + 1, 1, grams, v_top, v_bot)

    top, bottom = v_top[...], v_bot[...]
    lane = lanes((1, B))
    moved = pltpu.roll(top, SETS, 1)
    low = lane < SETS
    left = jnp.where(low, lane_gather(bottom, (SETS - lane) & (B - 1)), moved)
    right = jnp.where(low, moved, lane_gather(bottom, jnp.where(lane == B - 1, 0, (B + SETS - 1 - lane) & (B - 1))))
    return left, right


JACOBI_SCRATCH = [pltpu.VMEM((2, B + 16, B), F32) for _ in range(4)] + [pltpu.VMEM((2 * B, B), F32) for _ in range(2)]

ROWS = 4096
CHUNK = 512
CHUNKS = ROWS // CHUNK
MESH = pl.DeviceIdType.MESH
HBM = pl.BlockSpec(memory_space=pl.ANY)
WHOLE = pl.BlockSpec(memory_space=pltpu.VMEM)


def chunk(i):
    return pl.ds(pl.multiple_of(i * CHUNK, CHUNK), CHUNK)


def split(x):
    high = x.astype(BF16)
    return high, (x - high.astype(F32)).astype(BF16)


GRAM_SCRATCH = [pltpu.VMEM((2 * B, 4 * B), F32), pltpu.VMEM((8, 2 * B), F32)]


def gram_clear(products, squares):
    products[...] = jnp.zeros_like(products)
    squares[...] = jnp.zeros_like(squares)


def gram_add(x, products, squares):
    high, low = split(x)
    products[...] += lax.dot_general(
        high, jnp.concatenate([high, low], axis=1), (((0,), (0,)), ((), ())), preferred_element_type=F32
    )
    small = low.astype(F32)
    squares[...] += jnp.sum((small * small).reshape(x.shape[0] // 8, 8, 2 * B), axis=0)


def gram_blocks(products, squares, part):
    eye = lax.broadcasted_iota(jnp.int32, (B, B), 0) == lanes((B, B))
    low_square = jnp.sum(squares[...], axis=0, keepdims=True)
    ll = products[:B, 2 * B : 3 * B]
    lr = products[:B, 3 * B :]
    rl = products[B:, 2 * B : 3 * B]
    rr = products[B:, 3 * B :]
    part[:B, :] = products[:B, :B] + (ll + ll.T) + jnp.where(eye, low_square[:, :B], 0.0)
    part[B : 2 * B, :] = products[:B, B : 2 * B] + (lr + rl.T)
    part[2 * B :, :] = products[B:, B : 2 * B] + (rr + rr.T) + jnp.where(eye, low_square[:, B:], 0.0)


HALF = 3 * B // 2
SUM_SCRATCH = [
    pltpu.VMEM((HALF, B), F32),
    pltpu.VMEM((HALF, B), F32),
    pltpu.VMEM((HALF, B), F32),
    pltpu.VMEM((3 * B, B), F32),
    pltpu.SemaphoreType.DMA((3,)),
    pltpu.SemaphoreType.DMA((3,)),
]


def row_neighbours():
    pair, row = lax.axis_index("pair"), lax.axis_index("row")
    core, chip = lax.rem(row, 2), lax.div(row, 2)
    return core, (pair, 2 * chip + 1 - core), (pair, 2 * (1 - chip) + core)


def greet(devices):
    for device in devices:
        pl.semaphore_signal(pltpu.get_barrier_semaphore(), inc=1, device_id=device, device_id_type=MESH)


def remote(src, dst, send, recv, device):
    return pltpu.make_async_remote_copy(
        src_ref=src, dst_ref=dst, send_sem=send, recv_sem=recv, device_id=device, device_id_type=MESH
    )


def row_sum(part, recv_a, acc, recv_b, full, send, recv):
    core, mate, across = row_neighbours()
    mine, other = pl.ds(core * HALF, HALF), pl.ds((1 - core) * HALF, HALF)
    pl.semaphore_wait(pltpu.get_barrier_semaphore(), 2)
    first = remote(part.at[other, :], recv_a, send.at[0], recv.at[0], mate)
    first.start()
    first.wait()
    acc[...] = part[mine, :] + recv_a[...]
    second = remote(acc, recv_b, send.at[1], recv.at[1], across)
    second.start()
    second.wait()
    full[mine, :] = acc[...] + recv_b[...]
    third = remote(full.at[mine, :], full.at[mine, :], send.at[2], recv.at[2], mate)
    third.start()
    third.wait()


def round_kernel(count, *refs):
    ins, refs = refs[:count], refs[count:]
    left_out, right_out, x, v_high, v_low, load, store, part = refs[:8]
    gram, sums, solve = refs[8:10], refs[10:16], refs[16:]
    core, mate, across = row_neighbours()
    greet((mate, across))

    def loads(i):
        if count == 1:
            return [pltpu.make_async_copy(ins[0].at[chunk(i), :], x.at[chunk(i), :], load.at[i, 0])]
        return [
            pltpu.make_async_copy(ins[j].at[chunk(i), :], x.at[chunk(i), pl.ds(j * B, B)], load.at[i, j])
            for j in range(2)
        ]

    def stores(i):
        return [
            pltpu.make_async_copy(x.at[chunk(i), pl.ds(j * B, B)], out.at[chunk(i), :], store.at[i, j])
            for j, out in enumerate((left_out, right_out))
        ]

    @pl.loop(0, CHUNKS)
    def _(i):
        for c in loads(i):
            c.start()

    gram_clear(*gram)

    @pl.loop(0, CHUNKS)
    def _(i):
        for c in loads(i):
            c.wait()
        gram_add(x[chunk(i), :], *gram)

    gram_blocks(*gram, part)
    row_sum(part, *sums)
    full = sums[3]
    halves = jacobi(full[:B, :], full[B : 2 * B, :], full[2 * B :, :], solve[:4], *solve[4:])
    for j, half in enumerate(halves):
        v_high[:, j * B : (j + 1) * B], v_low[:, j * B : (j + 1) * B] = split(half)
    dot = functools.partial(jnp.dot, preferred_element_type=F32)

    @pl.loop(0, CHUNKS)
    def _(i):
        high, low = split(x[chunk(i), :])
        x[chunk(i), :] = dot(high, v_high[...]) + (dot(high, v_low[...]) + dot(low, v_high[...]))
        for c in stores(i):
            c.start()

    @pl.loop(0, CHUNKS)
    def _(i):
        for c in stores(i):
            c.wait()


def one_round(index, *ins):
    return pl.pallas_call(
        functools.partial(round_kernel, len(ins)),
        out_shape=(jax.ShapeDtypeStruct((ROWS, B), F32),) * 2,
        in_specs=[HBM] * len(ins),
        out_specs=(HBM, HBM),
        scratch_shapes=[
            pltpu.VMEM((ROWS, 2 * B), F32),
            pltpu.VMEM((2 * B, 2 * B), BF16),
            pltpu.VMEM((2 * B, 2 * B), BF16),
            pltpu.SemaphoreType.DMA((CHUNKS, 2)),
            pltpu.SemaphoreType.DMA((CHUNKS, 2)),
            pltpu.VMEM((3 * B, B), F32),
        ]
        + GRAM_SCRATCH
        + SUM_SCRATCH
        + JACOBI_SCRATCH,
        compiler_params=pltpu.CompilerParams(
            collective_id=index, has_side_effects=True, vmem_limit_bytes=VMEM_LIMIT
        ),
        cost_estimate=pl.CostEstimate(
            flops=10 * ROWS * (2 * B) ** 2, bytes_accessed=4 * ROWS * 2 * B * 2, transcendentals=0
        ),
        name="round",
    )(*ins)


LOW_BITS = 3
VMEM_LIMIT = 60 * 2**20


def transfer_kernel(mask, block, out, send, recv):
    to = (jnp.bitwise_xor(lax.axis_index("pair"), mask), lax.axis_index("row"))
    greet((to,))
    pl.semaphore_wait(pltpu.get_barrier_semaphore(), 1)
    copy = remote(block, out, send, recv, to)
    copy.start()
    copy.wait()


def transfer(mask, block):
    if mask == 0:
        return block
    return pl.pallas_call(
        functools.partial(transfer_kernel, mask),
        out_shape=jax.ShapeDtypeStruct(block.shape, block.dtype),
        in_specs=[HBM],
        out_specs=HBM,
        scratch_shapes=[pltpu.SemaphoreType.DMA, pltpu.SemaphoreType.DMA],
        compiler_params=pltpu.CompilerParams(collective_id=transfer_id(mask), has_side_effects=True),
        cost_estimate=pl.CostEstimate(flops=0, bytes_accessed=2 * ROWS * B * 4, transcendentals=0),
        name="transfer",
    )(block)


def transfer_id(mask):
    return 2 if mask == lax.axis_size("pair") - 1 else mask + 2


def route(block, mask):
    count = lax.axis_size("pair")
    low_count = 1 << LOW_BITS

    def high_part(high, block):
        return lax.switch(
            jnp.bitwise_and(mask, low_count - 1),
            [functools.partial(transfer, high * low_count + low) for low in range(low_count)],
            block,
        )

    return lax.switch(
        jnp.right_shift(mask, LOW_BITS), [functools.partial(high_part, h) for h in range(count // low_count)], block
    )


def local(matrix, plan):
    left, right = one_round(1, matrix[:, :B], matrix[:, B:])
    right = route(right, plan[0])
    left, right = one_round(1, left, right)
    return jnp.concatenate([left, route(right, plan[1])], axis=1)


def solution(mesh):
    return jax.shard_map(
        local, mesh=mesh, in_specs=(P("row", "pair"), P()), out_specs=P("row", "pair"), check_vma=False
    )
```

time: 297 us -> 223 us (0.75)
  Pallas kernels: 276 us -> 207 us
    pallas_call x2, Pallas kernels: 211 us -> 162 us  [transfer(): pl.pallas_call(functools.partial(transfer_kernel, mask), out_shape=jax.Sh...]
    pallas_call x2, Pallas kernels: 65.3 us -> 45.4 us  [one_round(): pl.pallas_call(functools.partial(round_kernel, len(ins)), out_shape=(jax....]
    unnamed x8 -> x4, local copies, waits for them, and re-layouts: 6.4 us -> 1.32 us
    slice x0 -> x1, local copies, waits for them, and re-layouts: none -> 4.48 us  [local(): left, right = one_round(1, matrix[:, :B], matrix[:, B:])]
where the time goes in v1:
time: 223 us
  Pallas kernels  207 us (93%)
  local copies, waits for them, and re-layouts  9.56 us (4%)
  other arithmetic  3.87 us (2%)
    pallas_call x2, Pallas kernels, transfer(): pl.pallas_call(functools.partial(transfer_kernel, mask), out_shape=jax.Sh...  162 us
    pallas_call x2, Pallas kernels, one_round(): pl.pallas_call(functools.partial(round_kernel, len(ins)), out_shape=(jax....  45.4 us
    slice x1, local copies, waits for them, and re-layouts, local(): left, right = one_round(1, matrix[:, :B], matrix[:, B:])  4.48 us

profile of v1, /device:TPU:1, one launch (start us, length us, event | category | flops | bytes accessed | tf_op | source)
XLA Modules:
  0.0 223.2 jit_solution(17340983484122684142)
XLA Ops:
  0.0 4.5 %fusion = (f32[4096,128]{1,0:T(8,128)}, f32[4096,128]{1,0:T(8,128)}) fusion(f32[4096,256]{1,0:T(8,128)} %param.146), kind=kLoop, calls=%fused_computation.1 | loop fusion | bytes 8388608 | tf_op jit(solution)/shard_map/slice | solution.py:329
  4.5 0.0 copy-start.1
  4.5 22.3 %round.2 = (f32[4096,128]{1,0:T(8,128)}, f32[4096,128]{1,0:T(8,128)S(1)}) custom-call(f32[4096,128]{1,0:T(8,128)} %get-tuple-element.400.refs_0_, f32[4096,128]{1,0:T(8,128)} %get-tuple-element.399.refs_1_), custom_call_target="tpu_custom_call" | custom-call | flops 2684354560 | bytes 8388608 | tf_op jit(solution)/shard_map/round/pallas_call | solution.py:254
  26.8 0.0 copy-done.1
  26.8 0.6 fusion.1
  28.1 64.4 %conditional.18 = (f32[4096,128]{1,0:T(8,128)S(1)}) conditional(s32[]{:T(128)} %clamp.54, (s32[]{:T(128)}, f32[4096,128]{1,0:T(8,128)S(1)}) %tuple.437, (s32[]{:T(128)}, f32[4096,128]{1,0:T(8,128)S(1)}) %tuple.437, (s32[]{:T(128)}, f32[4096,128]{1,0:T(8,128)S(1)}) %tuple.437, (s32[]{:T(128)}, ...), branch_computations={%region_0.0_spmd, %region_9.0_spmd, %region_18.0_spmd, %region_27.... | conditional | flops 2 | bytes 8388652 | solution.py:323
  28.8 62.1 %conditional.7 = (f32[4096,128]{1,0:T(8,128)}) conditional(s32[]{:T(128)} %clamp.43, f32[4096,128]{1,0:T(8,128)S(1)} %get-tuple-element.374, f32[4096,128]{1,0:T(8,128)S(1)} %get-tuple-element.374, f32[4096,128]{1,0:T(8,128)S(1)} %get-tuple-element.374, f32[4096,128]{1,0:T(8,128)S(1)} %get-tuple-element.374, ...), branch_computations={%region_64.0_spmd, %region_65.0_spmd, %region_66.0_spmd, %region_6... | conditional | bytes 4194312 | solution.py:317
  28.8 62.0 %transfer.181 = f32[4096,128]{1,0:T(8,128)} custom-call(f32[4096,128]{1,0:T(8,128)S(1)} %block.48), custom_call_target="tpu_custom_call" | custom-call | bytes 4194304 | tf_op jit(solution)/shard_map/cond/branch_7_fun/cond/branch_0_fun/transfer/pallas_call | solution.py:296
  90.9 1.6 copy.138
  92.5 0.0 copy-start
  92.5 1.3 copy-done
  93.8 23.0 %round.3 = (f32[4096,128]{1,0:T(8,128)}, f32[4096,128]{1,0:T(8,128)S(1)}) custom-call(f32[4096,128]{1,0:T(8,128)} %get-tuple-element.395.refs_0_, f32[4096,128]{1,0:T(8,128)} %copy-done), custom_call_target="tpu_custom_call" | custom-call | flops 2684354560 | bytes 8388608 | tf_op jit(solution)/shard_map/round/pallas_call | solution.py:254
  117.4 101.9 %conditional.19 = (f32[4096,128]{1,0:T(8,128)S(1)}) conditional(s32[]{:T(128)} %clamp.55, (s32[]{:T(128)}, f32[4096,128]{1,0:T(8,128)S(1)}) %tuple.438, (s32[]{:T(128)}, f32[4096,128]{1,0:T(8,128)S(1)}) %tuple.438, (s32[]{:T(128)}, f32[4096,128]{1,0:T(8,128)S(1)}) %tuple.438, (s32[]{:T(128)}, ...), branch_computations={%region_72.0_spmd, %region_81.0_spmd, %region_90.0_spmd, %region_9... | conditional | flops 2 | bytes 8388652 | solution.py:323
  118.0 99.7 %conditional.15 = (f32[4096,128]{1,0:T(8,128)}) conditional(s32[]{:T(128)} %clamp.51, f32[4096,128]{1,0:T(8,128)S(1)} %get-tuple-element.390, f32[4096,128]{1,0:T(8,128)S(1)} %get-tuple-element.390, f32[4096,128]{1,0:T(8,128)S(1)} %get-tuple-element.390, f32[4096,128]{1,0:T(8,128)S(1)} %get-tuple-element.390, ...), branch_computations={%region_136.0_spmd, %region_137.0_spmd, %region_138.0_spmd, %regio... | conditional | bytes 4194312 | solution.py:317
  118.1 99.7 %transfer.251 = f32[4096,128]{1,0:T(8,128)} custom-call(f32[4096,128]{1,0:T(8,128)S(1)} %block.111), custom_call_target="tpu_custom_call" | custom-call | bytes 4194304 | tf_op jit(solution)/shard_map/cond/branch_7_fun/cond/branch_7_fun/transfer/pallas_call | solution.py:296
  217.7 1.6 copy.146
  219.3 3.9 %pad_maximum_fusion = f32[4096,256]{1,0:T(8,128)} fusion(f32[4096,128]{1,0:T(8,128)S(1)} %get-tuple-element.420, f32[4096,128]{1,0:T(8,128)} %get-tuple-element.397), kind=kLoop, calls=%fused_computation | loop fusion | flops 1048576 | bytes 8388608 | tf_op jit(solution)/shard_map/concatenate | solution.py:332
Async XLA Ops:
  4.5 22.4 %copy-start.1 = (s32[2]{0:T(128)S(1)}, s32[2]{0:T(128)}, u32[]{:S(2)}) copy-start(s32[2]{0:T(128)} %param.147) | copy-start | bytes 28
  92.5 1.3 copy-start

commit v2 on v1

--- a/solution.py
+++ b/solution.py
@@ -121,33 +121,34 @@
     return high, (x - high.astype(F32)).astype(BF16)
 
 
-GRAM_SCRATCH = [pltpu.VMEM((2 * B, 4 * B), F32), pltpu.VMEM((8, 2 * B), F32)]
-
-
-def gram_clear(products, squares):
+GRAM_SCRATCH = [pltpu.VMEM((2 * B, 6 * B), F32)]
+
+
+def gram_clear(products):
     products[...] = jnp.zeros_like(products)
-    squares[...] = jnp.zeros_like(squares)
-
-
-def gram_add(x, products, squares):
-    high, low = split(x)
-    products[...] += lax.dot_general(
-        high, jnp.concatenate([high, low], axis=1), (((0,), (0,)), ((), ())), preferred_element_type=F32
-    )
-    small = low.astype(F32)
-    squares[...] += jnp.sum((small * small).reshape(x.shape[0] // 8, 8, 2 * B), axis=0)
-
-
-def gram_blocks(products, squares, part):
-    eye = lax.broadcasted_iota(jnp.int32, (B, B), 0) == lanes((B, B))
-    low_square = jnp.sum(squares[...], axis=0, keepdims=True)
+
+
+def gram_add(x, products):
+    high = x.astype(BF16)
+    rest = x - high.astype(F32)
+    middle, low = split(rest)
+    product = functools.partial(
+        lax.dot_general, dimension_numbers=(((0,), (0,)), ((), ())), preferred_element_type=F32
+    )
+    products[:, : 4 * B] += product(high, jnp.concatenate([high, middle], axis=1))
+    products[:, 2 * B : 4 * B] += product(high, low)
+    products[:, 4 * B :] += product(middle, middle)
+
+
+def gram_blocks(products, part):
+    whole = products[:, : 2 * B] + products[:, 4 * B :]
     ll = products[:B, 2 * B : 3 * B]
-    lr = products[:B, 3 * B :]
+    lr = products[:B, 3 * B : 4 * B]
     rl = products[B:, 2 * B : 3 * B]
-    rr = products[B:, 3 * B :]
-    part[:B, :] = products[:B, :B] + (ll + ll.T) + jnp.where(eye, low_square[:, :B], 0.0)
-    part[B : 2 * B, :] = products[:B, B : 2 * B] + (lr + rl.T)
-    part[2 * B :, :] = products[B:, B : 2 * B] + (rr + rr.T) + jnp.where(eye, low_square[:, B:], 0.0)
+    rr = products[B:, 3 * B : 4 * B]
+    part[:B, :] = whole[:B, :B] + (ll + ll.T)
+    part[B : 2 * B, :] = whole[:B, B:] + (lr + rl.T)
+    part[2 * B :, :] = whole[B:, B:] + (rr + rr.T)
 
 
 HALF = 3 * B // 2
@@ -198,7 +199,7 @@
 def round_kernel(count, *refs):
     ins, refs = refs[:count], refs[count:]
     left_out, right_out, x, v_high, v_low, load, store, part = refs[:8]
-    gram, sums, solve = refs[8:10], refs[10:16], refs[16:]
+    gram, sums, solve = refs[8:9], refs[9:15], refs[15:]
     core, mate, across = row_neighbours()
     greet((mate, across))
 
@@ -268,7 +269,7 @@
         + SUM_SCRATCH
         + JACOBI_SCRATCH,
         compiler_params=pltpu.CompilerParams(
-            collective_id=index, has_side_effects=True, vmem_limit_bytes=VMEM_LIMIT
+            collective_id=index, has_side_effects=True, vmem_limit_bytes=VMEM_LIMITS[len(ins) - 1]
         ),
         cost_estimate=pl.CostEstimate(
             flops=10 * ROWS * (2 * B) ** 2, bytes_accessed=4 * ROWS * 2 * B * 2, transcendentals=0
@@ -278,13 +279,14 @@
 
 
 LOW_BITS = 3
-VMEM_LIMIT = 60 * 2**20
+VMEM_LIMITS = (60 * 2**20, 40 * 2**20)
 
 
 def transfer_kernel(mask, block, out, send, recv):
     to = (jnp.bitwise_xor(lax.axis_index("pair"), mask), lax.axis_index("row"))
-    greet((to,))
-    pl.semaphore_wait(pltpu.get_barrier_semaphore(), 1)
+    if transfer_id(mask) is not None:
+        greet((to,))
+        pl.semaphore_wait(pltpu.get_barrier_semaphore(), 1)
     copy = remote(block, out, send, recv, to)
     copy.start()
     copy.wait()
@@ -305,8 +307,12 @@
     )(block)
 
 
+OWN_BARRIERS = 36
+
+
 def transfer_id(mask):
-    return 2 if mask == lax.axis_size("pair") - 1 else mask + 2
+    number = 3 if mask == lax.axis_size("pair") - 1 else mask + 3
+    return number if number <= OWN_BARRIERS else None
 
 
 def route(block, mask):
@@ -326,9 +332,9 @@
 
 
 def local(matrix, plan):
-    left, right = one_round(1, matrix[:, :B], matrix[:, B:])
+    left, right = one_round(1, matrix)
     right = route(right, plan[0])
-    left, right = one_round(1, left, right)
+    left, right = one_round(2, left, right)
     return jnp.concatenate([left, route(right, plan[1])], axis=1)
 
 

time: 223 us -> 210 us (0.942)
  Pallas kernels: 207 us -> 195 us
    pallas_call x2, Pallas kernels: 162 us -> 150 us  [transfer(): pl.pallas_call(functools.partial(transfer_kernel, mask), out_shape=jax.Sh...]
    slice x1 -> x0, local copies, waits for them, and re-layouts: 4.48 us -> none  [local(): left, right = one_round(1, matrix[:, :B], matrix[:, B:])]
where the time goes in v2:
time: 210 us
  Pallas kernels  195 us (93%)
  local copies, waits for them, and re-layouts  8.95 us (4%)
  other arithmetic  3.87 us (2%)
    pallas_call x2, Pallas kernels, transfer(): pl.pallas_call(functools.partial(transfer_kernel, mask), out_shape=jax.Sh...  150 us
    pallas_call x2, Pallas kernels, one_round(): pl.pallas_call(functools.partial(round_kernel, len(ins)), out_shape=(jax....  44.8 us
    cond x2, local copies, waits for them, and re-layouts  4.65 us

profile of v2, /device:TPU:1, one launch (start us, length us, event | category | flops | bytes accessed | tf_op | source)
XLA Modules:
  0.0 210.1 jit_solution(13012797409893934891)
XLA Ops:
  0.0 1.4 fusion
  1.4 23.4 %round.2 = (f32[4096,128]{1,0:T(8,128)}, f32[4096,128]{1,0:T(8,128)S(1)}) custom-call(f32[4096,256]{1,0:T(8,128)} %refs_0_.1), custom_call_target="tpu_custom_call" | custom-call | flops 2684354560 | bytes 8388608 | tf_op jit(solution)/shard_map/round/pallas_call | solution.py:255
  25.4 103.5 %conditional.18 = (f32[4096,128]{1,0:T(8,128)S(1)}) conditional(s32[]{:T(128)} %clamp.54, (s32[]{:T(128)}, f32[4096,128]{1,0:T(8,128)S(1)}) %tuple.437, (s32[]{:T(128)}, f32[4096,128]{1,0:T(8,128)S(1)}) %tuple.437, (s32[]{:T(128)}, f32[4096,128]{1,0:T(8,128)S(1)}) %tuple.437, (s32[]{:T(128)}, ...), branch_computations={%region_0.0_spmd, %region_9.0_spmd, %region_18.0_spmd, %region_27.... | conditional | flops 2 | bytes 8388652 | solution.py:329
  26.0 101.3 %conditional.7 = (f32[4096,128]{1,0:T(8,128)}) conditional(s32[]{:T(128)} %clamp.43, f32[4096,128]{1,0:T(8,128)S(1)} %get-tuple-element.374, f32[4096,128]{1,0:T(8,128)S(1)} %get-tuple-element.374, f32[4096,128]{1,0:T(8,128)S(1)} %get-tuple-element.374, f32[4096,128]{1,0:T(8,128)S(1)} %get-tuple-element.374, ...), branch_computations={%region_64.0_spmd, %region_65.0_spmd, %region_66.0_spmd, %region_6... | conditional | bytes 4194312 | solution.py:323
  26.1 101.2 %transfer.188 = f32[4096,128]{1,0:T(8,128)} custom-call(f32[4096,128]{1,0:T(8,128)S(1)} %block.55), custom_call_target="tpu_custom_call" | custom-call | bytes 4194304 | tf_op jit(solution)/shard_map/cond/branch_7_fun/cond/branch_7_fun/transfer/pallas_call | solution.py:298
  127.3 1.6 copy.138
  128.9 0.0 copy-start.1
  128.9 1.3 copy-done.1
  130.2 0.0 copy-start
  130.2 1.6 copy-done
  131.8 21.4 %round.3 = (f32[4096,128]{1,0:T(8,128)S(1)}, f32[4096,128]{1,0:T(8,128)}) custom-call(f32[4096,128]{1,0:T(8,128)S(1)} %copy-done, f32[4096,128]{1,0:T(8,128)} %copy-done.1), custom_call_target="tpu_custom_call" | custom-call | flops 2684354560 | bytes 8388608 | tf_op jit(solution)/shard_map/round/pallas_call | solution.py:255
  153.9 52.3 %conditional.19 = (f32[4096,128]{1,0:T(8,128)}) conditional(s32[]{:T(128)} %clamp.55, (s32[]{:T(128)}, f32[4096,128]{1,0:T(8,128)}) %tuple.438, (s32[]{:T(128)}, f32[4096,128]{1,0:T(8,128)}) %tuple.438, (s32[]{:T(128)}, f32[4096,128]{1,0:T(8,128)}) %tuple.438, (s32[]{:T(128)}, f32[4096,128]{1,0:T(8,128)}) %tuple.438, ...), branch_computations={%region_72.0_spmd, %region_81.0_spmd, %region_90.0_spmd, %region_9... | conditional | flops 2 | bytes 8388652 | solution.py:329
  154.6 48.5 %conditional.10 = (f32[4096,128]{1,0:T(8,128)}) conditional(s32[]{:T(128)} %clamp.46, f32[4096,128]{1,0:T(8,128)} %get-tuple-element.380, f32[4096,128]{1,0:T(8,128)} %get-tuple-element.380, f32[4096,128]{1,0:T(8,128)} %get-tuple-element.380, f32[4096,128]{1,0:T(8,128)} %get-tuple-element.380, ...), branch_computations={%region_91.0_spmd, %region_92.0_spmd, %region_93.0_spmd, %region_9... | conditional | bytes 4194312 | solution.py:323
  154.7 48.5 %transfer.205 = f32[4096,128]{1,0:T(8,128)} custom-call(f32[4096,128]{1,0:T(8,128)} %block.65), custom_call_target="tpu_custom_call" | custom-call | bytes 4194304 | tf_op jit(solution)/shard_map/cond/branch_2_fun/cond/branch_1_fun/transfer/pallas_call | solution.py:298
  203.2 3.1 %copy.141 = f32[4096,128]{1,0:T(8,128)} copy(f32[4096,128]{1,0:T(8,128)} %get-tuple-element.411) | data formatting | bytes 4194304 | tf_op jit(solution)/shard_map/cond
  206.2 3.9 %pad_maximum_fusion = f32[4096,256]{1,0:T(8,128)} fusion(f32[4096,128]{1,0:T(8,128)} %get-tuple-element.418, f32[4096,128]{1,0:T(8,128)S(1)} %get-tuple-element.397), kind=kLoop, calls=%fused_computation | loop fusion | flops 1048576 | bytes 8388608 | tf_op jit(solution)/shard_map/concatenate | solution.py:338
Async XLA Ops:
  128.9 1.3 copy-start.1
  130.2 1.6 copy-start
